TPU v7x, 32 devices: a whole 2x2x4 slice. The times are simulated.
32 devices in a mesh: groups: 2 (over y), pre: 4 (over z), post: 2 (over x), rep: 2 (over core).
Axes of the slice: x: 2, y: 2, z: 4, core: 2. Of those that a mesh axis runs over, the one named last changes fastest.
Arguments:
- rates0: bfloat16 [256, 2048], P(('groups', 'rep'), 'pre'), parts along dimension 0, may hold values from -0.94921875 to 0.94921875
- stimulus: bfloat16 [256, 2048], P(('groups', 'rep'), 'post'), parts along dimension 0, may hold values from -6 to 6
- cotangent: bfloat16 [256, 2048], P(('groups', 'rep'), 'post'), parts along dimension 0, may hold values from -6 to 6
- weights: bfloat16 [8, 2, 64, 128, 128], P(('groups', 'pre'), 'post'), parts along dimension 0, may hold values from -0.375 to 0.375
- src_block: int32 [8, 2, 64], P(('groups', 'pre'), 'post'), parts along dimension 0, may hold values from 0 to 3
- dst_block: int32 [8, 2, 64], P(('groups', 'pre'), 'post'), parts along dimension 0, may hold values from 0 to 7
- live_count: int32 [8, 2], P(('groups', 'pre'), 'post'), parts along dimension 0, may hold values from 16 to 64, as said below
- cell_type: int32 [4096], P(('groups', 'post')), parts along dimension 0, may hold values from 0 to 31
- gains: float32 [32], replicated, may hold values from 0.5 to 2
Outputs:
- final_rates: bfloat16 [256, 2048], P(('groups', 'rep'), 'post'), parts along dimension 0
- grad_weight: float32 [8, 2, 64, 128, 128], P(('groups', 'pre'), 'post', 'rep'), parts along dimension 0
- grad_gain: float32 [64], P('groups'), parts along dimension 0
There are 2 independent parts, one for each index of `groups`. A program takes and returns all parts, laid end to end along the dimension named above; an argument that names none is the same for every part. Nothing has to cross between parts.
Inputs may be any that keep to these rules, and one draw needn't show every extreme that they name: Slots from live_count on are unused; some tile of every draw uses all 64 slots.
All inputs are finite; a program needn't handle non-finite values.
Results may differ from a plain program's by a relative error of at most 0.035.
Values may be sent and summed in bfloat16 or wider, within the bound.
A program may use at most 64 MiB of HBM per device.

v0:
```python
import jax
import jax.numpy as jnp
from jax import lax
from jax.sharding import PartitionSpec as P

STEPS = 4


leak_rate = 0.35


def from_root(value, axis, source):
    kept = jnp.where(lax.axis_index(axis) == source, value, 0).astype(value.dtype)
    return lax.psum(kept, axis)


def spread_forward(rates_pre, blocks, sources, targets, post_blocks):
    rows = rates_pre.shape[0]
    width = blocks.shape[1]
    grid = rates_pre.reshape(rows, -1, width)
    picked = jnp.take(grid, sources, axis=1)
    prod = jnp.einsum("bkp,kpq->kbq", picked, blocks, preferred_element_type=jnp.float32)
    summed = jax.ops.segment_sum(prod, targets, num_segments=post_blocks)
    return jnp.transpose(summed, (1, 0, 2)).reshape(rows, post_blocks * width)


def spread_backward(delta_post, blocks, sources, targets, pre_blocks):
    rows = delta_post.shape[0]
    width = blocks.shape[1]
    grid = delta_post.reshape(rows, -1, width)
    picked = jnp.take(grid, targets, axis=1)
    prod = jnp.einsum("bkq,kpq->kbp", picked, blocks, preferred_element_type=jnp.float32)
    summed = jax.ops.segment_sum(prod, sources, num_segments=pre_blocks)
    return jnp.transpose(summed, (1, 0, 2)).reshape(rows, pre_blocks * width)


def block_grads(rates_pre, delta_post, sources, targets, width):
    rows = rates_pre.shape[0]
    picked_rates = jnp.take(rates_pre.reshape(rows, -1, width), sources, axis=1)
    picked_delta = jnp.take(delta_post.reshape(rows, -1, width), targets, axis=1)
    return jnp.einsum(
        "bkp,bkq->kpq", picked_rates, picked_delta, preferred_element_type=jnp.float32
    )


def body(rates0, stimulus, cotangent, weights, src_block, dst_block, live_count, cell_type, gains):
    pre_per_post = lax.axis_size("pre") // lax.axis_size("post")
    pre_index = lax.axis_index("pre")
    post_index = lax.axis_index("post")
    blocks = weights[0, 0]
    sources = src_block[0, 0]
    targets = dst_block[0, 0]
    slots = blocks.shape[0]
    width = blocks.shape[1]
    slot_mask = (jnp.arange(slots, dtype=jnp.int32) < live_count[0, 0]).astype(jnp.float32)
    used = blocks * slot_mask.astype(jnp.bfloat16)[:, None, None]
    n_pre = rates0.shape[1]
    n_post = stimulus.shape[1]
    fine_width = n_post // lax.axis_size("pre")
    pre_blocks = n_pre // width
    post_blocks = n_post // width

    def add_type(kind, total):
        return total + jnp.where(cell_type == kind, gains[kind], 0.0)

    gain_post = lax.fori_loop(0, gains.shape[0], add_type, jnp.zeros(cell_type.shape, jnp.float32))
    fine_types = lax.dynamic_slice_in_dim(cell_type, pre_index * fine_width, fine_width, 0)
    type_table = (
        fine_types[None, :] == jnp.arange(gains.shape[0], dtype=jnp.int32)[:, None]
    ).astype(jnp.float32)
    start_pieces = []
    for piece in range(pre_per_post):
        start_pieces.append(from_root(rates0, "pre", post_index * pre_per_post + piece))
    rates_post = jnp.concatenate(start_pieces, axis=1)
    stim_local = stimulus.astype(jnp.float32)
    rates_local = rates_post
    rates_pre = rates0
    saved_rates = []
    saved_act = []
    saved_cur = []
    for step in range(STEPS):
        partial_value = spread_forward(rates_pre, used, sources, targets, post_blocks)
        cur = lax.psum(partial_value.astype(jnp.bfloat16), "pre").astype(jnp.float32)
        act = jnp.tanh(gain_post * cur + stim_local)
        saved_rates.append(rates_pre)
        saved_act.append(act)
        saved_cur.append(cur)
        rates_local = (
            (1.0 - leak_rate) * rates_local.astype(jnp.float32) + leak_rate * act
        ).astype(jnp.bfloat16)
        rates_post = rates_local
        own_half = lax.dynamic_slice_in_dim(rates_post, pre_index % pre_per_post * n_pre, n_pre, 1)
        rates_pre = from_root(own_half, "post", pre_index // pre_per_post)
    error = cotangent.astype(jnp.float32)
    grad_blocks = jnp.zeros((slots, width, width), jnp.float32)
    type_grad = jnp.zeros(gains.shape, jnp.float32)
    for step in reversed(range(STEPS)):
        act = saved_act[step]
        du = error * leak_rate * (1.0 - act * act)
        local_values = jnp.sum(du * saved_cur[step], axis=0)
        weighted = lax.dynamic_slice_in_dim(
            local_values, pre_index * fine_width, fine_width, local_values.ndim - 1
        )
        type_part = jnp.sum(type_table * weighted[None, :], axis=1)
        type_grad = type_grad + lax.psum(type_part, ("pre", "post", "rep"))
        dcur_local = (du * gain_post).astype(jnp.bfloat16)
        grad_blocks = grad_blocks + block_grads(
            saved_rates[step], dcur_local, sources, targets, width
        )
        if step > 0:
            back_partial = spread_backward(dcur_local, used, sources, targets, pre_blocks)
            back_pre = lax.psum(back_partial.astype(jnp.bfloat16), "post").astype(jnp.float32)
            back_pieces = []
            for piece in range(pre_per_post):
                back_pieces.append(
                    from_root(
                        back_pre.astype(jnp.bfloat16), "pre", post_index * pre_per_post + piece
                    ).astype(back_pre.dtype)
                )
            back_post = jnp.concatenate(back_pieces, axis=1)
            error = (1.0 - leak_rate) * error + back_post
    grad_blocks = grad_blocks * slot_mask[:, None, None]
    grad_share = lax.psum_scatter(
        grad_blocks.astype(jnp.bfloat16), "rep", scatter_dimension=0, tiled=True
    ).astype(jnp.float32)
    return (rates_post, grad_share[None, None], type_grad)


def solution(mesh):
    return jax.shard_map(
        body,
        mesh=mesh,
        in_specs=(
            P(("groups", "rep"), "pre"),
            P(("groups", "rep"), "post"),
            P(("groups", "rep"), "post"),
            P(("groups", "pre"), "post", None, None, None),
            P(("groups", "pre"), "post", None),
            P(("groups", "pre"), "post", None),
            P(("groups", "pre"), "post"),
            P(("groups", "post")),
            P(),
        ),
        out_specs=(
            P(("groups", "rep"), "post"),
            P(("groups", "pre"), "post", "rep", None, None),
            P("groups"),
        ),
        check_vma=False,
    )
```

profile of v0, /device:TPU:3, one launch (start us, length us, event | category | flops | bytes accessed | tf_op | source)
XLA Modules:
  0.0 567.2 jit_solution(3508988603859013150)
XLA Ops:
  13.1 7.1 %scatter_fusion = f32[8,64,128]{2,1,0:T(8,128)S(1)} fusion(f32[8,64,128]{2,1,0:T(8,128)S(1)} %broadcast.43.clone.1, s32[64]{0:T(128)S(1)} %bitcast.150, f32[64,64,128]{2,1,0:T(8,128)} %fusion.23), kind=kCustom, calls=%fused_computation.8 | custom fusion | flops 524288 | bytes 6291712 | tf_op jit(solution)/shard_map/scatter-add | solution.py:23
  22.4 61.7 %while.14 = (s32[]{:T(128)}, f32[1024]{0:T(1024)S(1)}, s32[1024]{0:T(1024)S(1)}, f32[32]{0:T(128)}, s32[]{:T(128)}, /*index=5*/s32[]{:T(128)}) while((s32[]{:T(128)}, f32[1024]{0:T(1024)S(1)}, s32[1024]{0:T(1024)S(1)}, f32[32]{0:T(128)}, s32[]{:T(128)}, /*index=5*/s32[]{:T(128)}) %tuple.87), condition=%wide.region_3.4_spmd.clone, body=%wide.region_2.3_spmd.clone.sunk | while | flops 4099 | bytes 12395 | solution.py:66
  86.6 20.5 %all-reduce.18.cloned.1.call-done = bf16[64,4,128]{2,0,1:T(8,128)(2,1)} async-done(((bf16[64,4,128]{2,0,1:T(8,128)(2,1)}), bf16[64,4,128]{2,0,1:T(8,128)(2,1)}) %all-reduce.18.cloned.1.call-update) | async-done | bytes 65552 | tf_op jit(solution)/shard_map/psum | solution.py:14
  113.1 7.2 %scatter_fusion.1 = f32[8,64,128]{2,1,0:T(8,128)S(1)} fusion(f32[8,64,128]{2,1,0:T(8,128)S(1)} %broadcast.43.clone.2, s32[64]{0:T(128)} %bitcast.147, f32[64,64,128]{2,1,0:T(8,128)} %fusion.20), kind=kCustom, calls=%fused_computation.9 | custom fusion | flops 524288 | bytes 6291712 | tf_op jit(solution)/shard_map/scatter-add | solution.py:23
  121.0 34.1 %all-reduce.20.cloned.1.call-done = bf16[64,1024]{1,0:T(8,128)(2,1)} async-done(((bf16[64,1024]{1,0:T(8,128)(2,1)}), bf16[64,1024]{1,0:T(8,128)(2,1)}) %all-reduce.20.cloned.1.call-update) | async-done | bytes 131088 | tf_op jit(solution)/shard_map/psum | solution.py:83
  157.5 21.2 %all-reduce.22.cloned.1.call-done = bf16[64,4,128]{2,0,1:T(8,128)(2,1)} async-done(((bf16[64,4,128]{2,0,1:T(8,128)(2,1)}), bf16[64,4,128]{2,0,1:T(8,128)(2,1)}) %all-reduce.22.cloned.1.call-update) | async-done | bytes 65552 | tf_op jit(solution)/shard_map/psum | solution.py:14
  184.6 7.2 %scatter_fusion.2 = f32[8,64,128]{2,1,0:T(8,128)S(1)} fusion(f32[8,64,128]{2,1,0:T(8,128)S(1)} %broadcast.43.clone, s32[64]{0:T(128)} %bitcast.148, f32[64,64,128]{2,1,0:T(8,128)} %fusion.17), kind=kCustom, calls=%fused_computation.10 | custom fusion | flops 524288 | bytes 6291712 | tf_op jit(solution)/shard_map/scatter-add | solution.py:23
  192.6 34.1 %all-reduce.24.cloned.1.call-done = bf16[64,1024]{1,0:T(8,128)(2,1)} async-done(((bf16[64,1024]{1,0:T(8,128)(2,1)}), bf16[64,1024]{1,0:T(8,128)(2,1)}) %all-reduce.24.cloned.1.call-update) | async-done | bytes 131088 | tf_op jit(solution)/shard_map/psum | solution.py:83
  230.2 20.1 %all-reduce.26.cloned.1.call-done = bf16[64,4,128]{2,0,1:T(8,128)(2,1)} async-done(((bf16[64,4,128]{2,0,1:T(8,128)(2,1)}), bf16[64,4,128]{2,0,1:T(8,128)(2,1)}) %all-reduce.26.cloned.1.call-update) | async-done | bytes 65552 | tf_op jit(solution)/shard_map/psum | solution.py:14
  256.3 7.2 %scatter_fusion.3 = f32[8,64,128]{2,1,0:T(8,128)S(1)} fusion(f32[8,64,128]{2,1,0:T(8,128)S(1)} %broadcast.43, s32[64]{0:T(128)} %bitcast.149, f32[64,64,128]{2,1,0:T(8,128)} %fusion.14), kind=kCustom, calls=%fused_computation.11 | custom fusion | flops 524288 | bytes 6291712 | tf_op jit(solution)/shard_map/scatter-add | solution.py:23
  264.9 33.4 %all-reduce.28.cloned.1.call-done = bf16[64,1024]{1,0:T(8,128)(2,1)} async-done(((bf16[64,1024]{1,0:T(8,128)(2,1)}), bf16[64,1024]{1,0:T(8,128)(2,1)}) %all-reduce.28.cloned.1.call-update) | async-done | bytes 131088 | tf_op jit(solution)/shard_map/psum | solution.py:83
  305.2 7.3 %scatter_fusion.4 = f32[4,64,128]{2,1,0:T(8,128)S(1)} fusion(f32[4,64,128]{2,1,0:T(8,128)S(1)} %broadcast.46.clone, s32[64]{0:T(128)} %bitcast.151, f32[64,64,128]{2,1,0:T(8,128)} %fusion.9), kind=kCustom, calls=%fused_computation.12 | custom fusion | flops 524288 | bytes 6291712 | tf_op jit(solution)/shard_map/scatter-add | solution.py:33
  313.2 21.0 %all-reduce.30.cloned.1.call-done = bf16[64,512]{1,0:T(8,128)(2,1)} async-done(((bf16[64,512]{1,0:T(8,128)(2,1)}), bf16[64,512]{1,0:T(8,128)(2,1)}) %all-reduce.30.cloned.1.call-update) | async-done | bytes 65552 | tf_op jit(solution)/shard_map/psum | solution.py:112
  335.8 35.7 %all-reduce.40.cloned.1.call-done = (bf16[64,512]{1,0:T(8,128)(2,1)}, bf16[64,512]{1,0:T(8,128)(2,1)}) async-done(((bf16[64,512]{1,0:T(8,128)(2,1)}, bf16[64,512]{1,0:T(8,128)(2,1)}), (bf16[64,512]{1,0:T(8,128)(2,1)}, bf16[64,512]{1,0:T(8,128)(2,1)})) %all-reduce.40.cloned.1.call-update) | async-done | bytes 131088 | tf_op jit(solution)/shard_map/psum | solution.py:14
  378.5 7.2 %scatter_fusion.5 = f32[4,64,128]{2,1,0:T(8,128)S(1)} fusion(f32[4,64,128]{2,1,0:T(8,128)S(1)} %broadcast.46.clone.1, s32[64]{0:T(128)} %bitcast.152, f32[64,64,128]{2,1,0:T(8,128)} %fusion.5), kind=kCustom, calls=%fused_computation.13 | custom fusion | flops 524288 | bytes 6291712 | tf_op jit(solution)/shard_map/scatter-add | solution.py:33
  386.4 20.8 %all-reduce.32.cloned.1.call-done = bf16[64,512]{1,0:T(8,128)(2,1)} async-done(((bf16[64,512]{1,0:T(8,128)(2,1)}), bf16[64,512]{1,0:T(8,128)(2,1)}) %all-reduce.32.cloned.1.call-update) | async-done | bytes 65552 | tf_op jit(solution)/shard_map/psum | solution.py:112
  409.0 4.4 fusion.11
  413.4 31.3 %all-reduce.38.cloned.1.call-done = (bf16[64,512]{1,0:T(8,128)(2,1)}, bf16[64,512]{1,0:T(8,128)(2,1)}) async-done(((bf16[64,512]{1,0:T(8,128)(2,1)}, bf16[64,512]{1,0:T(8,128)(2,1)}), (bf16[64,512]{1,0:T(8,128)(2,1)}, bf16[64,512]{1,0:T(8,128)(2,1)})) %all-reduce.38.cloned.1.call-update) | async-done | bytes 131088 | tf_op jit(solution)/shard_map/psum | solution.py:14
  453.5 7.1 %scatter_fusion.6 = f32[4,64,128]{2,1,0:T(8,128)S(1)} fusion(f32[4,64,128]{2,1,0:T(8,128)S(1)} %broadcast.46, s32[64]{0:T(128)S(1)} %bitcast.153, f32[64,64,128]{2,1,0:T(8,128)} %fusion.1), kind=kCustom, calls=%fused_computation.14 | custom fusion | flops 524288 | bytes 6291712 | tf_op jit(solution)/shard_map/scatter-add | solution.py:33
  465.6 16.5 %all-reduce.34.cloned.1.call-done = bf16[64,512]{1,0:T(8,128)(2,1)} async-done(((bf16[64,512]{1,0:T(8,128)(2,1)}), bf16[64,512]{1,0:T(8,128)(2,1)}) %all-reduce.34.cloned.1.call-update) | async-done | bytes 65552 | tf_op jit(solution)/shard_map/psum | solution.py:112
  483.7 4.2 fusion.3
  487.9 31.5 %all-reduce.36.cloned.1.call-done = (bf16[64,512]{1,0:T(8,128)(2,1)}, bf16[64,512]{1,0:T(8,128)(2,1)}) async-done(((bf16[64,512]{1,0:T(8,128)(2,1)}, bf16[64,512]{1,0:T(8,128)(2,1)}), (bf16[64,512]{1,0:T(8,128)(2,1)}, bf16[64,512]{1,0:T(8,128)(2,1)})) %all-reduce.36.cloned.1.call-update) | async-done | bytes 131088 | tf_op jit(solution)/shard_map/psum | solution.py:14
  521.4 6.5 %multiply_convert_fusion = bf16[64,128,128]{2,1,0:T(8,128)(2,1)} fusion(f32[64,128,128]{2,1,0:T(8,128)} %fusion.3, f32[64,128,128]{2,1,0:T(8,128)} %fusion.11, f32[64,128,128]{2,1,0:T(8,128)} %fusion.7, f32[64]{0:T(128)S(1)} %copy-done.22, bf16[64,64,128]{2,1,0:T(8,128)(2,1)S(1)} %gather_fusion.7, pred[64]{0:T(512)(128)(4,1)S(1)} %get-tuple-element.138, ...), kind=kOutput, calls=%fused_computation.16 | convolution fusion | flops 140509184 | bytes 16777600 | tf_op jit(solution)/shard_map/bkp,bkq->kpq/dot_general | solution.py:41
  530.5 27.4 %psum.178 = f32[32]{0:T(128)} all-reduce(f32[32]{0:T(128)S(1)} %add_add_fusion), channel_id=1, replica_groups=mesh['groups'=2,'pre'=4,'post'=2,'rep'=2] {'pre','post','rep'}, use_global_device_ids=true, to_apply=%region_30.33 | all-reduce | flops 32 | bytes 256 | tf_op jit(solution)/shard_map/psum | solution.py:105
  (202 shorter events, 138.6 us)
Async XLA Ops:
  7.2 77.0 %all-reduce.42.cloned.1.call-start = ((), (), s32[]{:S(2)}) async-start(), calls=%async_computation.14 | async-start | bytes 524288 | tf_op jit(solution)/shard_map/psum | solution.py:83
  9.3 172.0 %copy-start.15 = (bf16[64]{0:T(256)(128)(2,1)}, bf16[64]{0:T(256)(128)(2,1)S(1)}, u32[]{:S(2)}) copy-start(bf16[64]{0:T(256)(128)(2,1)S(1)} %get-tuple-element.137) | copy-start | bytes 388
  13.1 71.1 %copy-start.3 = (bf16[64,1024]{1,0:T(8,128)(2,1)S(1)}, bf16[64,1024]{1,0:T(8,128)(2,1)}, u32[]{:S(2)}) copy-start(bf16[64,1024]{1,0:T(8,128)(2,1)} %param.16) | copy-start | bytes 393220
  22.4 84.7 %all-reduce.18.cloned.1.call-start = ((), (), s32[]{:S(2)}) async-start(), calls=%async_computation.1 | async-start | bytes 131072 | tf_op jit(solution)/shard_map/psum | solution.py:14
  86.5 68.6 %all-reduce.20.cloned.1.call-start = ((), (), s32[]{:S(2)}) async-start(), calls=%async_computation.2 | async-start | bytes 262144 | tf_op jit(solution)/shard_map/psum | solution.py:83
  121.0 57.7 %all-reduce.22.cloned.1.call-start = ((), (), s32[]{:S(2)}) async-start(), calls=%async_computation.3 | async-start | bytes 131072 | tf_op jit(solution)/shard_map/psum | solution.py:14
  157.5 69.2 %all-reduce.24.cloned.1.call-start = ((), (), s32[]{:S(2)}) async-start(), calls=%async_computation.4 | async-start | bytes 262144 | tf_op jit(solution)/shard_map/psum | solution.py:83
  192.5 60.5 %copy-start.16 = (bf16[64]{0:T(256)(128)(2,1)S(1)}, bf16[64]{0:T(256)(128)(2,1)}, u32[]{:S(2)}) copy-start(bf16[64]{0:T(256)(128)(2,1)} %copy-done.15) | copy-start | bytes 388
  192.5 57.8 %all-reduce.26.cloned.1.call-start = ((), (), s32[]{:S(2)}) async-start(), calls=%async_computation.5 | async-start | bytes 131072 | tf_op jit(solution)/shard_map/psum | solution.py:14
  229.0 69.3 %all-reduce.28.cloned.1.call-start = ((), (), s32[]{:S(2)}) async-start(), calls=%async_computation.6 | async-start | bytes 262144 | tf_op jit(solution)/shard_map/psum | solution.py:83
  264.2 36.9 %copy-start.17 = (bf16[64]{0:T(256)(128)(2,1)S(1)}, bf16[64]{0:T(256)(128)(2,1)}, u32[]{:S(2)}) copy-start(bf16[64]{0:T(256)(128)(2,1)} %copy-done.15) | copy-start | bytes 388
  264.2 70.1 %all-reduce.30.cloned.1.call-start = ((), (), s32[]{:S(2)}) async-start(), calls=%async_computation.7 | async-start | bytes 131072 | tf_op jit(solution)/shard_map/psum | solution.py:112
  264.9 40.3 %copy-start.20 = (s32[1024]{0:T(1024)}, s32[1024]{0:T(1024)S(1)}, u32[]{:S(2)}) copy-start(s32[1024]{0:T(1024)S(1)} %pad_clamp_fusion) | copy-start | bytes 12292
  305.2 66.4 %copy-start.4 = (bf16[64,1024]{1,0:T(8,128)(2,1)S(1)}, bf16[64,1024]{1,0:T(8,128)(2,1)}, u32[]{:S(2)}) copy-start(bf16[64,1024]{1,0:T(8,128)(2,1)} %param.17) | copy-start | bytes 393220
  313.2 58.4 %all-reduce.40.cloned.1.call-start = ((), (), s32[]{:S(2)}) async-start(), calls=%async_computation.13 | async-start | bytes 262144 | tf_op jit(solution)/shard_map/psum | solution.py:14
  335.8 71.4 %all-reduce.32.cloned.1.call-start = ((), (), s32[]{:S(2)}) async-start(), calls=%async_computation.8 | async-start | bytes 131072 | tf_op jit(solution)/shard_map/psum | solution.py:112
  386.4 58.3 %all-reduce.38.cloned.1.call-start = ((), (), s32[]{:S(2)}) async-start(), calls=%async_computation.12 | async-start | bytes 262144 | tf_op jit(solution)/shard_map/psum | solution.py:14
  408.7 36.0 %copy-start.5 = (bf16[64,1024]{1,0:T(8,128)(2,1)S(1)}, bf16[64,1024]{1,0:T(8,128)(2,1)}, u32[]{:S(2)}) copy-start(bf16[64,1024]{1,0:T(8,128)(2,1)} %all-reduce.24.cloned.1.call-done) | copy-start | bytes 393220
  408.7 73.3 %all-reduce.34.cloned.1.call-start = ((), (), s32[]{:S(2)}) async-start(), calls=%async_computation.9 | async-start | bytes 131072 | tf_op jit(solution)/shard_map/psum | solution.py:112
  461.3 58.1 %all-reduce.36.cloned.1.call-start = ((), (), s32[]{:S(2)}) async-start(), calls=%async_computation.11 | async-start | bytes 262144 | tf_op jit(solution)/shard_map/psum | solution.py:14
  483.6 35.8 %copy-start.9 = (bf16[64,512]{1,0:T(8,128)(2,1)S(1)}, bf16[64,512]{1,0:T(8,128)(2,1)}, u32[]{:S(2)}) copy-start(bf16[64,512]{1,0:T(8,128)(2,1)} %get-tuple-element.119) | copy-start | bytes 196612
  483.6 35.8 %copy-start.10 = (bf16[64,512]{1,0:T(8,128)(2,1)S(1)}, bf16[64,512]{1,0:T(8,128)(2,1)}, u32[]{:S(2)}) copy-start(bf16[64,512]{1,0:T(8,128)(2,1)} %get-tuple-element.120) | copy-start | bytes 196612
  483.6 35.8 %copy-start.11 = (bf16[64,1024]{1,0:T(8,128)(2,1)S(1)}, bf16[64,1024]{1,0:T(8,128)(2,1)}, u32[]{:S(2)}) copy-start(bf16[64,1024]{1,0:T(8,128)(2,1)} %get-tuple-element.121) | copy-start | bytes 393220
  483.6 74.3 %reduce-scatter.2.cloned.1.call-start = ((), (), s32[]{:S(2)}) async-start(), calls=%async_computation.10 | async-start | bytes 3145728 | tf_op jit(solution)/shard_map/reduce_scatter | solution.py:123
  (13 other events, 160.3 us)
Sparse Core Ops, SparseCore 0:
  22.5 34.9 all-reduce.41
  86.7 20.3 all-reduce.17
  121.1 33.9 all-reduce.19
  157.8 20.8 all-reduce.21
  192.6 33.9 all-reduce.23
  229.4 20.8 all-reduce.25
  264.3 33.9 all-reduce.27
  313.3 20.8 all-reduce.29
  337.2 34.3 all-reduce.39
  386.5 20.6 all-reduce.31
  410.3 34.3 all-reduce.37
  461.4 20.6 all-reduce.33
  485.0 34.3 all-reduce.35
  528.0 11.8 reduce-scatter.1
where the time goes:
time: 577 us; the launch traced here: 567 us
  waiting for transfers between devices  320 us (55%)
  other arithmetic  98.4 us (17%)
  local copies, waits for them, and re-layouts  60.8 us (11%)
  matrix products  43.7 us (8%)
  blocking collectives  27.4 us (5%)
  between operations  15.2 us (3%)
    psum x6, waiting for transfers between devices, from_root(): return lax.psum(kept, axis)  160 us
    psum x4, waiting for transfers between devices, body(): lax.psum(partial_value.astype(jnp.bfloat16), 'pre').astype(jnp.float32)  102 us
    psum x3, waiting for transfers between devices, body(): lax.psum(back_partial.astype(jnp.bfloat16), 'post').astype(jnp.float32)  58.3 us
    dynamic_slice x32, local copies, waits for them, and re-layouts, add_type(): return total + jnp.where(cell_type == kind, gains[kind], 0.0)  40.4 us
    scatter-add x4, other arithmetic, spread_forward(): summed = jax.ops.segment_sum(prod, targets, num_segments=post_blocks)  28.6 us
    psum x1, blocking collectives, body(): type_grad = type_grad + lax.psum(type_part, ('pre', 'post', 'rep'))  27.4 us
    scatter-add x3, other arithmetic, spread_backward(): summed = jax.ops.segment_sum(prod, sources, num_segments=pre_blocks)  21.6 us
    add x32, other arithmetic, add_type(): return total + jnp.where(cell_type == kind, gains[kind], 0.0)  20.4 us
  transfers between devices with their start and end apart: 14, of which 12 were waited for; matrix products, arithmetic and copies ran while one was open for 14% of the time, Pallas kernels for 0%

commit v1 on v0

v1 whole, which is shorter than its diff:
```python
import functools

import jax
import jax.numpy as jnp
from jax import lax
from jax.experimental import pallas as pl
from jax.experimental.pallas import tpu as pltpu
from jax.sharding import PartitionSpec as P

STEPS = 4
LEAK = 0.35
MESH = pl.DeviceIdType.MESH
F32 = jnp.float32
BF16 = jnp.bfloat16
CHUNK = 8


def build_kernel(src_ref, dst_ref, live_ref, w_ref, out_ref, acc):
    width = w_ref.shape[-1]
    part = pl.program_id(0)

    @pl.when(part == 0)
    def _():
        acc[...] = jnp.zeros_like(acc)

    live = live_ref[0, 0]
    for s in range(CHUNK):
        k = part * CHUNK + s

        @pl.when(k < live)
        def _():
            rows = pl.ds(pl.multiple_of(src_ref[0, 0, k] * width, width), width)
            cols = pl.ds(pl.multiple_of(dst_ref[0, 0, k] * width, width), width)
            acc[rows, cols] += w_ref[0, 0, s].astype(F32)

    @pl.when(part == pl.num_programs(0) - 1)
    def _():
        out_ref[...] = acc[...].astype(BF16)


def emit_kernel(src_ref, dst_ref, live_ref, g_ref, out_ref, zero, sem):
    width = zero.shape[0]
    share = out_ref.shape[2]
    first = lax.axis_index("rep") * share
    live = live_ref[0, 0]
    zero[...] = jnp.zeros_like(zero)

    def start(k, carry):
        slot = first + k

        @pl.when(slot < live)
        def _():
            rows = pl.ds(pl.multiple_of(src_ref[0, 0, slot] * width, width), width)
            cols = pl.ds(pl.multiple_of(dst_ref[0, 0, slot] * width, width), width)
            pltpu.make_async_copy(g_ref.at[rows, cols], out_ref.at[0, 0, k], sem.at[k]).start()

        @pl.when(slot >= live)
        def _():
            pltpu.make_async_copy(zero, out_ref.at[0, 0, k], sem.at[k]).start()

        return carry

    lax.fori_loop(0, share, start, 0)

    def finish(k, carry):
        pltpu.make_async_copy(zero, out_ref.at[0, 0, k], sem.at[k]).wait()
        return carry

    lax.fori_loop(0, share, finish, 0)


def step_kernel(
    sizes,
    rates_ref, stim_ref, cot_ref, w_ref, ct_ref, gains_ref,
    final_ref, gg_ref, g_ref,
    rbuf, dbuf, fbuf, psend, precv, dsend, bsend, brecv, stage, sbuf, ctsend, ctbuf, grecv, acts, curs,
    s_sem, s_rsem, p_sem, p_rsem, r_sem, r_rsem, d_sem, d_rsem, b_sem, b_rsem, f_sem, f_rsem,
    xr_sem, xr_rsem, xd_sem, xd_rsem, g_sem, g_rsem,
):
    pre, post, rep, chains, rh, n_pre = sizes
    ppp = pre // post
    rows = post * rh
    i, j, c = lax.axis_index("pre"), lax.axis_index("post"), lax.axis_index("rep")
    a_me = lax.rem(i, ppp)
    j_me = lax.div(i, ppp)
    home = j_me == j
    away = jnp.logical_not(home)
    group = pre * post * rep
    me = (i * post + j) * rep + c

    def where_is(flat):
        return {
            "pre": lax.div(flat, post * rep),
            "post": lax.rem(lax.div(flat, rep), post),
            "rep": lax.rem(flat, rep),
        }

    def peer(n):
        return lax.rem(me + n, group)

    barrier = pltpu.get_barrier_semaphore()

    def greet(n, carry):
        pl.semaphore_signal(barrier, inc=1, device_id=where_is(peer(n)), device_id_type=MESH)
        return carry

    lax.fori_loop(1, group, greet, 0)

    def copy(src, dst, send, recv, to):
        return pltpu.make_async_remote_copy(
            src_ref=src, dst_ref=dst, send_sem=send, recv_sem=recv, device_id=to, device_id_type=MESH
        )

    def flat_rows(value, lead):
        if rh % 16 == 0:
            return value.reshape(lead * rh, value.shape[-1])
        value = value.astype(F32)
        return value.reshape(lead * rh, value.shape[-1]).astype(BF16)

    mine = pl.ds(pl.multiple_of(a_me * n_pre, n_pre), n_pre)
    for which, ref in enumerate((stim_ref, cot_ref)):
        value = ref[:, mine].astype(F32)
        for ch in range(chains):
            for h in range(post):
                top = ch * rows + h * rh
                stage[which, ch, h] = value[top:top + rh].astype(BF16)
    ctsend[...] = jnp.broadcast_to(ct_ref[:, mine], ctsend.shape)
    start_rates = rates_ref[...].astype(F32)
    for ch in range(chains):
        for h in range(post):
            top = ch * rows + h * rh
            rbuf[0, 0, ch, h] = start_rates[top:top + rh].astype(BF16)

    pl.semaphore_wait(barrier, group - 1)

    def share_copies(h):
        to = {"post": h}
        yield copy(stage.at[0, :, h], sbuf.at[0], s_sem.at[h, 0], s_rsem.at[0], to)
        yield copy(stage.at[1, :, h], sbuf.at[1], s_sem.at[h, 1], s_rsem.at[1], to)
        yield copy(ctsend, ctbuf, s_sem.at[h, 2], s_rsem.at[2], to)

    for h in range(post):
        @pl.when(jnp.logical_and(home, h != j))
        def _():
            for one in share_copies(h):
                one.start()

    @pl.when(home)
    def _():
        for which in range(2):
            for ch in range(chains):
                sbuf[which, ch] = stage[which, ch, j]
        ctbuf[...] = ctsend[...]

    other = {"rep": 1 - c}

    def swap_rates(t, ch):
        return copy(rbuf.at[0, t, ch], rbuf.at[1, t, ch], xr_sem.at[t, ch], xr_rsem.at[t, ch], other)

    def swap_delta(t, ch, a):
        return copy(
            dbuf.at[0, a, t, ch], dbuf.at[1, a, t, ch], xd_sem.at[t, ch, a], xd_rsem.at[t, ch, a], other
        )

    def part_copy(t, ch, a, h):
        return copy(
            psend.at[t, ch, a, h], precv.at[t, ch, i], p_sem.at[t, ch, a, h], p_rsem.at[t, ch, i],
            {"pre": ppp * j + a, "post": h},
        )

    def is_me(m, h):
        return jnp.logical_and(m == i, h == j)

    def rate_copy(t, ch, d):
        return copy(
            rbuf.at[0, t, ch, j], rbuf.at[0, t, ch, j], r_sem.at[t, ch, d], r_rsem.at[t, ch, j],
            {"post": lax.rem(j + d, post)},
        )

    def delta_copy(t, ch, to_i):
        return copy(
            dsend.at[t, ch], dbuf.at[0, a_me, t, ch, j], d_sem.at[t, ch, to_i], d_rsem.at[t, ch, a_me, j],
            {"pre": to_i, "post": j_me},
        )

    def final_copy(ch, to_i):
        return copy(
            fbuf.at[1, ch, 0, 0], fbuf.at[0, ch, a_me, j], f_sem.at[ch, to_i], f_rsem.at[ch, a_me, j],
            {"pre": to_i, "post": j_me},
        )

    def back_copy(t, ch, d):
        h = lax.rem(j + d, post)
        return copy(
            bsend.at[t, ch, h], brecv.at[t, ch, j], b_sem.at[t, ch, d], b_rsem.at[t, ch, j], {"post": h}
        )

    def wait_slot(ref, sem):
        copy(ref, ref, sem, sem, other).wait_recv()

    gain = None
    for t in range(STEPS):
        for ch in range(chains):
            if t > 0:
                for d in range(1, post):
                    h = lax.rem(j + d, post)
                    wait_slot(rbuf.at[0, t, ch, h], r_rsem.at[t, ch, h])
            now = flat_rows(rbuf[0, t, ch], post)
            for a in range(ppp):
                part = jnp.dot(now, w_ref[:, a * n_pre:(a + 1) * n_pre], preferred_element_type=F32)
                for h in range(post):
                    psend[t, ch, a, h] = part[h * rh:(h + 1) * rh].astype(BF16)
                for h in range(post):
                    self_here = is_me(ppp * j + a, h)

                    @pl.when(jnp.logical_not(self_here))
                    def _():
                        part_copy(t, ch, a, h).start()

                    @pl.when(self_here)
                    def _():
                        precv[t, ch, i] = psend[t, ch, a, h]

            swap_rates(t, ch).start()
        if t == 0:
            @pl.when(away)
            def _():
                wait_slot(sbuf.at[0], s_rsem.at[0])
                wait_slot(sbuf.at[1], s_rsem.at[1])
                wait_slot(ctbuf, s_rsem.at[2])

            types = ctbuf[...]
            gain = jnp.zeros(types.shape, F32)
            for k in range(gains_ref.shape[0]):
                gain = jnp.where(types == k, gains_ref[k], gain)
            gain = gain[0:1]
        for ch in range(chains):
            cur = None
            for m in range(pre):
                remote = jnp.logical_or(away, m != i)

                @pl.when(remote)
                def _():
                    wait_slot(precv.at[t, ch, m], p_rsem.at[t, ch, m])

                term = precv[t, ch, m].astype(F32)
                cur = term if cur is None else cur + term
            act = jnp.tanh(gain * cur + sbuf[0, ch].astype(F32))
            acts[t, ch] = act
            curs[t, ch] = cur
            fresh = ((1.0 - LEAK) * rbuf[0, t, ch, j].astype(F32) + LEAK * act).astype(BF16)
            if t < STEPS - 1:
                rbuf[0, t + 1, ch, j] = fresh
                for d in range(1, post):
                    rate_copy(t + 1, ch, d).start()
            else:
                fbuf[1, ch, 0, 0] = fresh

    errors = [sbuf[1, ch].astype(F32) for ch in range(chains)]
    tally = jnp.zeros((8, n_pre), F32)
    for t in reversed(range(STEPS)):
        for ch in range(chains):
            error = errors[ch]
            if t < STEPS - 1:
                total = bsend[t + 1, ch, j].astype(F32)
                for d in range(1, post):
                    h = lax.rem(j + d, post)
                    wait_slot(brecv.at[t + 1, ch, h], b_rsem.at[t + 1, ch, h])
                    total = total + brecv[t + 1, ch, h].astype(F32)
                error = (1.0 - LEAK) * error + total
            errors[ch] = error
            act = acts[t, ch]
            du = error * LEAK * (1.0 - act * act)
            dsend[t, ch] = (du * gain).astype(BF16)
            for m in range(pre):
                remote = jnp.logical_or(away, m != i)

                @pl.when(remote)
                def _():
                    delta_copy(t, ch, m).start()

            @pl.when(home)
            def _():
                dbuf[0, a_me, t, ch, j] = dsend[t, ch]

            weighed = du * curs[t, ch]
            for top in range(0, rh, 8):
                tally = tally + weighed[top:top + 8]
        if t == 0:
            break
        for ch in range(chains):
            for a in range(ppp):
                for h in range(post):
                    @pl.when(jnp.logical_not(is_me(ppp * j + a, h)))
                    def _():
                        wait_slot(dbuf.at[0, a, t, ch, h], d_rsem.at[t, ch, a, h])

            back = None
            for a in range(ppp):
                term = lax.dot_general(
                    flat_rows(dbuf[0, a, t, ch], post), w_ref[:, a * n_pre:(a + 1) * n_pre],
                    (((1,), (1,)), ((), ())), preferred_element_type=F32,
                )
                back = term if back is None else back + term
            for h in range(post):
                bsend[t, ch, h] = back[h * rh:(h + 1) * rh].astype(BF16)
            for d in range(1, post):
                back_copy(t, ch, d).start()
            for a in range(ppp):
                swap_delta(t, ch, a).start()

    kinds = grecv.shape[-1]
    hot = (lax.broadcasted_iota(jnp.int32, (kinds, n_pre), 0) == ctbuf[0:1]).astype(F32)
    grecv[me] = lax.dot_general(
        tally, hot, (((1,), (1,)), ((), ())), preferred_element_type=F32, precision=lax.Precision.HIGHEST
    )

    def gain_copy(n):
        return copy(grecv.at[me], grecv.at[me], g_sem.at[n], g_rsem.at[me], where_is(peer(n)))

    def send_gain(n, carry):
        gain_copy(n).start()
        return carry

    lax.fori_loop(1, group, send_gain, 0)

    for ch in range(chains):
        for m in range(pre):
            @pl.when(jnp.logical_or(away, m != i))
            def _():
                final_copy(ch, m).start()

        @pl.when(home)
        def _():
            fbuf[0, ch, a_me, j] = fbuf[1, ch, 0, 0]

    for t in range(1, STEPS):
        for ch in range(chains):
            swap_rates(t, ch).wait_recv()
            for a in range(ppp):
                swap_delta(t, ch, a).wait_recv()
    for ch in range(chains):
        swap_rates(0, ch).wait_recv()

    def outer(side, low, high, a):
        lead = (high - low) * chains * post
        return lax.dot_general(
            flat_rows(rbuf[side, low:high], lead), flat_rows(dbuf[side, a, low:high], lead),
            (((0,), (0,)), ((), ())), preferred_element_type=F32,
        )

    for a in range(ppp):
        cols = slice(a * n_pre, (a + 1) * n_pre)
        g_ref[:, cols] = outer(0, 1, STEPS, a) + outer(1, 1, STEPS, a)
    for ch in range(chains):
        for a in range(ppp):
            for h in range(post):
                @pl.when(jnp.logical_not(is_me(ppp * j + a, h)))
                def _():
                    wait_slot(dbuf.at[0, a, 0, ch, h], d_rsem.at[0, ch, a, h])

            swap_delta(0, ch, a).start()
    for a in range(ppp):
        cols = slice(a * n_pre, (a + 1) * n_pre)
        for ch in range(chains):
            swap_delta(0, ch, a).wait_recv()
        g_ref[:, cols] += outer(0, 0, 1, a) + outer(1, 0, 1, a)

    for ch in range(chains):
        for a in range(ppp):
            for h in range(post):
                @pl.when(jnp.logical_not(is_me(ppp * j + a, h)))
                def _():
                    wait_slot(fbuf.at[0, ch, a, h], f_rsem.at[ch, a, h])

            final_ref[ch * rows:(ch + 1) * rows, a * n_pre:(a + 1) * n_pre] = flat_rows(fbuf[0, ch, a], post)

    def take_gain(n, carry):
        source = peer(n)
        wait_slot(grecv.at[source], g_rsem.at[source])
        return carry

    lax.fori_loop(1, group, take_gain, 0)
    gathered = grecv[0]
    for n in range(1, group):
        gathered = gathered + grecv[n]
    gg_ref[...] = jnp.sum(gathered, axis=0, keepdims=True)

    for h in range(post):
        @pl.when(jnp.logical_and(home, h != j))
        def _():
            for one in share_copies(h):
                one.wait_send()

    for t in range(STEPS):
        for ch in range(chains):
            swap_rates(t, ch).wait_send()
            for a in range(ppp):
                swap_delta(t, ch, a).wait_send()
                for h in range(post):
                    @pl.when(jnp.logical_not(is_me(ppp * j + a, h)))
                    def _():
                        part_copy(t, ch, a, h).wait_send()

            for m in range(pre):
                @pl.when(jnp.logical_or(away, m != i))
                def _():
                    delta_copy(t, ch, m).wait_send()
                    if t == 0:
                        final_copy(ch, m).wait_send()

            if t > 0:
                for d in range(1, post):
                    rate_copy(t, ch, d).wait_send()
                    back_copy(t, ch, d).wait_send()

    def end_gain(n, carry):
        gain_copy(n).wait_send()
        return carry

    lax.fori_loop(1, group, end_gain, 0)


def body(rates0, stimulus, cotangent, weights, src_block, dst_block, live_count, cell_type, gains):
    pre, post, rep = lax.axis_size("pre"), lax.axis_size("post"), lax.axis_size("rep")
    batch, n_pre = rates0.shape
    n_post = stimulus.shape[1]
    slots, width = weights.shape[2], weights.shape[3]
    ppp = pre // post
    chains = 2 if batch // (2 * post) >= 16 else 1
    rh = batch // (chains * post)
    group = pre * post * rep
    smem = pl.BlockSpec(memory_space=pltpu.SMEM)
    vmem = pl.BlockSpec(memory_space=pltpu.VMEM)

    dense = pl.pallas_call(
        build_kernel,
        grid=(slots // CHUNK,),
        out_shape=jax.ShapeDtypeStruct((n_pre, n_post), BF16),
        in_specs=[smem, smem, smem, pl.BlockSpec((1, 1, CHUNK, width, width), lambda p: (0, 0, p, 0, 0))],
        out_specs=pl.BlockSpec((n_pre, n_post), lambda p: (0, 0)),
        scratch_shapes=[pltpu.VMEM((n_pre, n_post), F32)],
        compiler_params=pltpu.CompilerParams(vmem_limit_bytes=32 * 2**20),
        name="dense_tile",
    )(src_block, dst_block, live_count, weights)

    dma = pltpu.SemaphoreType.DMA
    V = pltpu.VMEM
    final, gain_grad, dense_grad = pl.pallas_call(
        functools.partial(step_kernel, (pre, post, rep, chains, rh, n_pre)),
        out_shape=(
            jax.ShapeDtypeStruct((batch, n_post), BF16),
            jax.ShapeDtypeStruct((1, 128), F32),
            jax.ShapeDtypeStruct((n_pre, n_post), F32),
        ),
        in_specs=[vmem, vmem, vmem, vmem, vmem, smem],
        out_specs=(vmem, vmem, vmem),
        scratch_shapes=[
            V((2, STEPS, chains, post, rh, n_pre), BF16),
            V((2, ppp, STEPS, chains, post, rh, n_pre), BF16),
            V((2, chains, ppp, post, rh, n_pre), BF16),
            V((STEPS, chains, ppp, post, rh, n_pre), BF16),
            V((STEPS, chains, pre, rh, n_pre), BF16),
            V((STEPS, chains, rh, n_pre), BF16),
            V((STEPS, chains, post, rh, n_pre), BF16),
            V((STEPS, chains, post, rh, n_pre), BF16),
            V((2, chains, post, rh, n_pre), BF16),
            V((2, chains, rh, n_pre), BF16),
            V((8, n_pre), jnp.int32),
            V((8, n_pre), jnp.int32),
            V((group, 8, 128), F32),
            V((STEPS, chains, rh, n_pre), F32),
            V((STEPS, chains, rh, n_pre), F32),
            dma((post, 3)), dma((3,)),
            dma((STEPS, chains, ppp, post)), dma((STEPS, chains, pre)),
            dma((STEPS, chains, post)), dma((STEPS, chains, post)),
            dma((STEPS, chains, pre)), dma((STEPS, chains, ppp, post)),
            dma((STEPS, chains, post)), dma((STEPS, chains, post)),
            dma((chains, pre)), dma((chains, ppp, post)),
            dma((STEPS, chains)), dma((STEPS, chains)),
            dma((STEPS, chains, ppp)), dma((STEPS, chains, ppp)),
            dma((group,)), dma((group,)),
        ],
        compiler_params=pltpu.CompilerParams(
            collective_id=0, has_side_effects=True, vmem_limit_bytes=48 * 2**20
        ),
        name="window",
    )(rates0, stimulus, cotangent, dense, cell_type.reshape(1, n_post), gains)

    share = slots // rep
    grad = pl.pallas_call(
        emit_kernel,
        out_shape=jax.ShapeDtypeStruct((1, 1, share, width, width), F32),
        in_specs=[smem, smem, smem, vmem],
        out_specs=pl.BlockSpec(memory_space=pl.ANY),
        scratch_shapes=[V((width, width), F32), dma((share,))],
        compiler_params=pltpu.CompilerParams(vmem_limit_bytes=32 * 2**20),
        name="emit_slots",
    )(src_block, dst_block, live_count, dense_grad)
    return final, grad, gain_grad[0, :gains.shape[0]]


def solution(mesh):
    return jax.shard_map(
        body,
        mesh=mesh,
        in_specs=(
            P(("groups", "rep"), "pre"),
            P(("groups", "rep"), "post"),
            P(("groups", "rep"), "post"),
            P(("groups", "pre"), "post", None, None, None),
            P(("groups", "pre"), "post", None),
            P(("groups", "pre"), "post", None),
            P(("groups", "pre"), "post"),
            P(("groups", "post")),
            P(),
        ),
        out_specs=(
            P(("groups", "rep"), "post"),
            P(("groups", "pre"), "post", "rep", None, None),
            P("groups"),
        ),
        check_vma=False,
    )
```

time: 577 us -> 79.1 us (0.14); the launches traced: 567 us -> 79.1 us
  waiting for transfers between devices: 320 us -> 0 us
  other arithmetic: 98.4 us -> 0 us
  Pallas kernels: 0 us -> 73.6 us
  local copies, waits for them, and re-layouts: 60.8 us -> 4.09 us
  matrix products: 43.7 us -> 0 us
  blocking collectives: 27.4 us -> 0 us
  between operations: 15.2 us -> 1.4 us
    psum x13 -> x0, waiting for transfers between devices: 320 us -> none  [the longest x6 160 us: from_root(): return lax.psum(kept, axis)]
    pallas_call x0 -> x3, Pallas kernels: none -> 73.6 us  [the longest x1 69.8 us: body(): pl.pallas_call(functools.partial(step_kernel, (pre, post, rep, chains, rh...]
    scatter-add x7 -> x0, other arithmetic: 50.2 us -> none  [the longest x4 28.6 us: spread_forward(): summed = jax.ops.segment_sum(prod, targets, num_segments=post_blocks)]
    dot_general x11 -> x0, matrix products: 43.7 us -> none  [the longest x4 19.4 us: block_grads(): jnp.einsum('bkp,bkq->kpq', picked_rates, picked_delta, preferred_element_...]
    dynamic_slice x37 -> x0, local copies, waits for them, and re-layouts: 42.8 us -> none  [the longest x32 40.4 us: add_type(): return total + jnp.where(cell_type == kind, gains[kind], 0.0)]
    psum x1 -> x0, blocking collectives: 27.4 us -> none  [body(): type_grad = type_grad + lax.psum(type_part, ('pre', 'post', 'rep'))]
    add x33 -> x0, other arithmetic: 20.4 us -> none  [the longest x32 20.4 us: add_type(): return total + jnp.where(cell_type == kind, gains[kind], 0.0)]
    gather x8 -> x0, local copies, waits for them, and re-layouts: 14.9 us -> none  [the longest x4 8.73 us: spread_forward(): picked = jnp.take(grid, sources, axis=1)]
  transfers between devices with their start and end apart: 14 -> 0, of which waited for: 12 -> 0; matrix products, arithmetic and copies ran while one was open for 14% -> 0% of each run, Pallas kernels for 0% -> 0%
where the time goes in v1:
time: 79.1 us
  Pallas kernels  73.6 us (93%)
  local copies, waits for them, and re-layouts  4.09 us (5%)
  between operations  1.4 us (2%)
    pallas_call x1, Pallas kernels, body(): pl.pallas_call(functools.partial(step_kernel, (pre, post, rep, chains, rh...  69.8 us
    unnamed x21, local copies, waits for them, and re-layouts  3.58 us
    pallas_call x1, Pallas kernels, body(): pl.pallas_call(emit_kernel, out_shape=jax.ShapeDtypeStruct((1, 1, share,...  2.13 us
    pallas_call x1, Pallas kernels, body(): pl.pallas_call(build_kernel, grid=(slots // CHUNK,), out_shape=jax.ShapeD...  1.65 us

profile of v1, /device:TPU:3, one launch (start us, length us, event | category | flops | bytes accessed | tf_op | source)
XLA Modules:
  0.0 79.1 jit_solution(15736979195815975194)
XLA Ops:
  0.6 0.0 copy-start.9
  1.3 0.0 copy-start
  1.3 1.6 %copy-done = bf16[1,1,64,128,128]{4,3,2,1,0:T(8,128)(2,1)S(1)} copy-done((bf16[1,1,64,128,128]{4,3,2,1,0:T(8,128)(2,1)S(1)}, bf16[1,1,64,128,128]{4,3,2,1,0:T(8,128)(2,1)}, u32[]{:S(2)}) %copy-start) | copy-done | bytes 2097176
  2.9 0.0 copy-start.5
  2.9 0.7 copy-done.5
  3.6 0.0 copy-start.7
  3.6 0.7 copy-done.7
  4.2 0.0 copy-start.2
  4.2 0.0 copy-start.3
  4.2 0.0 copy-start.4
  4.2 0.0 copy-start.6
  4.2 0.0 copy-start.8
  4.2 1.6 %dense_tile.1.w_ref = bf16[512,1024]{1,0:T(8,128)(2,1)S(1)} custom-call(s32[1,1,64]{2,1,0:T(1,128)S(1)} %copy-done.5, s32[1,1,64]{2,1,0:T(1,128)S(1)} %copy-done.7, s32[1,1]{1,0:T(1,128)S(6)} %copy.13.live_ref, bf16[1,1,64,128,128]{4,3,2,1,0:T(8,128)(2,1)S(1)} %copy-done), custom_call_target="tpu_custom_call" | custom-call | tf_op jit(solution)/shard_map/dense_tile/pallas_call | solution.py:436
  5.9 0.0 copy-done.9
  5.9 0.0 copy-done.1
  5.9 0.0 copy-done.2
  5.9 0.0 copy-done.3
  5.9 0.0 copy-done.4
  5.9 69.8 %window.1 = (bf16[64,1024]{1,0:T(8,128)(2,1)S(1)}, f32[1,128]{1,0:T(1,128)S(1)}, f32[512,1024]{1,0:T(8,128)S(1)}) custom-call(bf16[64,512]{1,0:T(8,128)(2,1)S(1)} %copy-done.3, bf16[64,1024]{1,0:T(8,128)(2,1)S(1)} %copy-done.1, bf16[64,1024]{1,0:T(8,128)(2,1)S(1)} %copy-done.2, bf16[512,1024]{1,0:T(8,128)(2,1)S(1)} %dense_tile.1.w_ref, ...), custom_call_target="tpu_custom_call" | custom-call | tf_op jit(solution)/shard_map/window/pallas_call | solution.py:449
  75.7 0.5 slice_bitcast_fusion
  76.3 0.0 copy-done.6
  76.3 0.0 copy-done.8
  76.3 2.1 %emit_slots.1 = f32[1,1,32,128,128]{4,3,2,1,0:T(8,128)} custom-call(s32[1,1,64]{2,1,0:T(1,128)S(1)} %copy-done.6, s32[1,1,64]{2,1,0:T(1,128)S(1)} %copy-done.8, s32[1,1]{1,0:T(1,128)S(6)} %copy.13.live_ref, f32[512,1024]{1,0:T(8,128)S(1)} %get-tuple-element.7.g_ref), custom_call_target="tpu_custom_call" | custom-call | tf_op jit(solution)/shard_map/emit_slots/pallas_call | solution.py:491
  78.4 0.7 copy.14
  (1 shorter events, 0.0 us)
Async XLA Ops:
  0.6 5.3 %copy-start.9 = (f32[32]{0:T(128)S(1)}, f32[32]{0:T(128)}, u32[]{:S(2)}) copy-start(f32[32]{0:T(128)} %gains_ref.1) | copy-start | bytes 388
  1.3 1.6 %copy-start = (bf16[1,1,64,128,128]{4,3,2,1,0:T(8,128)(2,1)S(1)}, bf16[1,1,64,128,128]{4,3,2,1,0:T(8,128)(2,1)}, u32[]{:S(2)}) copy-start(bf16[1,1,64,128,128]{4,3,2,1,0:T(8,128)(2,1)} %w_ref.1) | copy-start | bytes 6291460
  2.9 0.7 copy-start.5
  3.6 0.7 copy-start.7
  4.2 1.7 %copy-start.1 = (bf16[64,1024]{1,0:T(8,128)(2,1)S(1)}, bf16[64,1024]{1,0:T(8,128)(2,1)}, u32[]{:S(2)}) copy-start(bf16[64,1024]{1,0:T(8,128)(2,1)} %stim_ref.1) | copy-start | bytes 393220
  4.2 1.7 %copy-start.2 = (bf16[64,1024]{1,0:T(8,128)(2,1)S(1)}, bf16[64,1024]{1,0:T(8,128)(2,1)}, u32[]{:S(2)}) copy-start(bf16[64,1024]{1,0:T(8,128)(2,1)} %cot_ref.1) | copy-start | bytes 393220
  4.2 1.7 %copy-start.3 = (bf16[64,512]{1,0:T(8,128)(2,1)S(1)}, bf16[64,512]{1,0:T(8,128)(2,1)}, u32[]{:S(2)}) copy-start(bf16[64,512]{1,0:T(8,128)(2,1)} %rates_ref.1) | copy-start | bytes 196612
  4.2 1.7 %copy-start.4 = (s32[1024]{0:T(1024)S(1)}, s32[1024]{0:T(1024)}, u32[]{:S(2)}) copy-start(s32[1024]{0:T(1024)} %param.16) | copy-start | bytes 12292
  4.2 72.0 %copy-start.6 = (s32[1,1,64]{2,1,0:T(1,128)S(1)}, s32[1,1,64]{2,1,0:T(1,128)}, u32[]{:S(2)}) copy-start(s32[1,1,64]{2,1,0:T(1,128)} %src_ref.3) | copy-start | bytes 772
  4.2 72.0 %copy-start.8 = (s32[1,1,64]{2,1,0:T(1,128)S(1)}, s32[1,1,64]{2,1,0:T(1,128)}, u32[]{:S(2)}) copy-start(s32[1,1,64]{2,1,0:T(1,128)} %dst_ref.3) | copy-start | bytes 772

commit v2 on v1

v2 whole, which is shorter than its diff:
```python
import functools

import jax
import jax.numpy as jnp
from jax import lax
from jax.experimental import pallas as pl
from jax.experimental.pallas import tpu as pltpu
from jax.sharding import PartitionSpec as P

STEPS = 4
LEAK = 0.35
MESH = pl.DeviceIdType.MESH
F32 = jnp.float32
BF16 = jnp.bfloat16
CHUNK = 8


def build_kernel(src_ref, dst_ref, live_ref, w_ref, out_ref, acc):
    width = w_ref.shape[-1]
    part = pl.program_id(0)

    @pl.when(part == 0)
    def _():
        acc[...] = jnp.zeros_like(acc)

    live = live_ref[0, 0]
    for s in range(CHUNK):
        k = part * CHUNK + s

        @pl.when(k < live)
        def _():
            rows = pl.ds(pl.multiple_of(src_ref[0, 0, k] * width, width), width)
            block = dst_ref[0, 0, k]
            across = acc.shape[2] // width
            cols = pl.ds(pl.multiple_of(lax.rem(block, across) * width, width), width)
            acc[lax.div(block, across), rows, cols] += w_ref[0, 0, s].astype(F32)

    @pl.when(part == pl.num_programs(0) - 1)
    def _():
        out_ref[...] = acc[...].astype(BF16)


def emit_kernel(src_ref, dst_ref, live_ref, g_ref, out_ref, zero, sem):
    width = zero.shape[0]
    share = out_ref.shape[2]
    first = lax.axis_index("rep") * share
    live = live_ref[0, 0]
    zero[...] = jnp.zeros_like(zero)

    def start(k, carry):
        slot = first + k

        @pl.when(slot < live)
        def _():
            rows = pl.ds(pl.multiple_of(src_ref[0, 0, slot] * width, width), width)
            cols = pl.ds(pl.multiple_of(dst_ref[0, 0, slot] * width, width), width)
            pltpu.make_async_copy(g_ref.at[rows, cols], out_ref.at[0, 0, k], sem.at[k]).start()

        @pl.when(slot >= live)
        def _():
            pltpu.make_async_copy(zero, out_ref.at[0, 0, k], sem.at[k]).start()

        return carry

    lax.fori_loop(0, share, start, 0)

    def finish(k, carry):
        pltpu.make_async_copy(zero, out_ref.at[0, 0, k], sem.at[k]).wait()
        return carry

    lax.fori_loop(0, share, finish, 0)


def step_kernel(
    sizes,
    rates_ref, stim_ref, cot_ref, w_ref, ct_ref, gains_ref,
    final_ref, gg_ref, g_ref,
    wbuf, rbuf, dbuf, dz, fbuf, psend, precv, dsend, stage, sbuf, ctsend, ctbuf, grecv, acts, curs,
    w_sem, w_rsem, wx_sem, wx_rsem,
    s_sem, s_rsem, p_sem, p_rsem, r_sem, r_rsem, z_sem, z_rsem, q_sem, q_rsem, d_sem, d_rsem, f_sem, f_rsem,
    xd_sem, xd_rsem, g_sem, g_rsem,
):
    pre, post, rep, chains, rh, n_pre = sizes
    ppp = pre // post
    rows = chains * rh
    i, j, c = lax.axis_index("pre"), lax.axis_index("post"), lax.axis_index("rep")
    a_me = lax.rem(i, ppp)
    j_me = lax.div(i, ppp)
    home = j_me == j
    away = jnp.logical_not(home)
    group = pre * post * rep
    me = (i * post + j) * rep + c

    def where_is(flat):
        return {
            "pre": lax.div(flat, post * rep),
            "post": lax.rem(lax.div(flat, rep), post),
            "rep": lax.rem(flat, rep),
        }

    def peer(n):
        return lax.rem(me + n, group)

    barrier = pltpu.get_barrier_semaphore()

    def greet(n, carry):
        pl.semaphore_signal(barrier, inc=1, device_id=where_is(peer(n)), device_id_type=MESH)
        return carry

    lax.fori_loop(1, group, greet, 0)

    def copy(src, dst, send, recv, to):
        return pltpu.make_async_remote_copy(
            src_ref=src, dst_ref=dst, send_sem=send, recv_sem=recv, device_id=to, device_id_type=MESH
        )

    def flat_rows(value, lead):
        if rh % 16 == 0:
            return value.reshape(lead * rh, value.shape[-1])
        value = value.astype(F32)
        return value.reshape(lead * rh, value.shape[-1]).astype(BF16)

    def one_block(value):
        return value

    mine = pl.ds(pl.multiple_of(a_me * n_pre, n_pre), n_pre)
    for which, ref in enumerate((stim_ref, cot_ref)):
        value = ref[:, mine].astype(F32)
        for ch in range(chains):
            for h in range(post):
                top = h * rows + ch * rh
                stage[which, h, ch] = value[top:top + rh].astype(BF16)
    ctsend[...] = jnp.broadcast_to(ct_ref[:, mine], ctsend.shape)
    start_rates = rates_ref[...].astype(F32)
    for h in range(post):
        @pl.when(h == j)
        def _():
            for ch in range(chains):
                top = h * rows + ch * rh
                rbuf[0, 0, ch, h] = start_rates[top:top + rh].astype(BF16)

    half = n_pre // rep
    band = pl.ds(pl.multiple_of(c * half, half), half)
    other = {"rep": 1 - c}

    def weight_copy(d, a):
        to = {"post": lax.rem(j + d, post)}
        slot = j * ppp + a
        return copy(w_ref.at[a, band], wbuf.at[slot, band], w_sem.at[d, a], w_rsem.at[slot], to)

    def weight_swap(h, a):
        slot = h * ppp + a
        there = wbuf.at[slot, band]
        return copy(there, there, wx_sem.at[slot], wx_rsem.at[slot], other)

    pl.semaphore_wait(barrier, group - 1)

    def share_copies(h):
        to = {"post": h}
        yield copy(stage.at[0, h], sbuf.at[0], s_sem.at[h, 0], s_rsem.at[0], to)
        yield copy(stage.at[1, h], sbuf.at[1], s_sem.at[h, 1], s_rsem.at[1], to)
        yield copy(ctsend, ctbuf, s_sem.at[h, 2], s_rsem.at[2], to)

    for h in range(post):
        @pl.when(jnp.logical_and(home, h != j))
        def _():
            for one in share_copies(h):
                one.start()

    @pl.when(home)
    def _():
        for which in range(2):
            for ch in range(chains):
                sbuf[which, ch] = stage[which, j, ch]
        ctbuf[...] = ctsend[...]


    def swap_delta(t, ch, a):
        return copy(
            dbuf.at[0, a, t, ch], dbuf.at[1, a, t, ch], xd_sem.at[ch, a], xd_rsem.at[ch, a], other
        )

    def part_copy(t, ch, m):
        return copy(
            psend.at[t, ch, m], precv.at[t, ch, i], p_sem.at[t, ch, m], p_rsem.at[t, ch, i], {"pre": m}
        )

    def first_copy(ch, a, h):
        return copy(
            psend.at[0, ch, a * post + h], precv.at[0, ch, i], p_sem.at[0, ch, a * post + h],
            p_rsem.at[0, ch, i], {"pre": ppp * j + a, "post": h},
        )

    def cross(n):
        return lax.rem(j + n // rep, post), n % rep

    def spread_rates(t, ch, n):
        h, side = cross(n)
        to = {"post": h, "rep": lax.rem(c + side, rep)}
        return copy(
            rbuf.at[0, t, ch, j], rbuf.at[side, t, ch, j], r_sem.at[t, ch, n], r_rsem.at[side, t, ch, j], to
        )

    def spread_delta(t, ch, a, n):
        h, side = cross(n)
        to = {"post": h, "rep": lax.rem(c + side, rep)}
        return copy(
            dz.at[t, ch, h * ppp + a], dbuf.at[side, a, t, ch, j], q_sem.at[t, ch, a, n],
            q_rsem.at[side, a, t, ch, j], to,
        )

    def gather_copy(t, ch, d):
        return copy(
            dz.at[t, ch, i], dz.at[t, ch, i], z_sem.at[t, ch, d], z_rsem.at[t, ch, i],
            {"pre": lax.rem(i + d, pre)},
        )

    def is_me(m, h):
        return jnp.logical_and(m == i, h == j)

    def delta_copy(t, ch, to_i):
        return copy(
            dsend.at[ch], dbuf.at[0, a_me, t, ch, j], d_sem.at[ch, to_i], d_rsem.at[ch, a_me, j],
            {"pre": to_i, "post": j_me},
        )

    def final_copy(ch, to_i):
        return copy(
            fbuf.at[1, 0, 0, ch], fbuf.at[0, a_me, j, ch], f_sem.at[ch, to_i], f_rsem.at[ch, a_me, j],
            {"pre": to_i, "post": j_me},
        )

    def wait_slot(ref, sem):
        copy(ref, ref, sem, sem, other).wait_recv()

    gain = None
    def send_part(t, ch, m, now):
        psend[t, ch, m] = jnp.dot(now, wbuf[m], preferred_element_type=F32).astype(BF16)
        part_copy(t, ch, m).start()

    def own_part(t, ch, now):
        precv[t, ch, i] = jnp.dot(now, wbuf[i], preferred_element_type=F32).astype(BF16)

    reach = [d for d in range(2, pre)] + [1]
    for t in range(STEPS):
        if t == 0:
            for a in range(ppp):
                part = jnp.dot(rates_ref[...], w_ref[a], preferred_element_type=F32)
                for h in range(post):
                    for ch in range(chains):
                        top = h * rows + ch * rh
                        value = part[top:top + rh].astype(BF16)
                        here = is_me(ppp * j + a, h)

                        @pl.when(here)
                        def _():
                            precv[0, ch, i] = value

                        @pl.when(jnp.logical_not(here))
                        def _():
                            psend[0, ch, a * post + h] = value
                            first_copy(ch, a, h).start()

            for d in range(1, post):
                for a in range(ppp):
                    weight_copy(d, a).start()
            for a in range(ppp):
                wbuf[j * ppp + a] = w_ref[a]
        elif t == 1:
            nexts = [one_block(rbuf[0, 1, ch, j]) for ch in range(chains)]
            for d in range(post):
                h = lax.rem(j + d, post)
                if d > 0:
                    for a in range(ppp):
                        wait_slot(wbuf.at[h * ppp + a, band], w_rsem.at[h * ppp + a])
                        weight_swap(h, a).start()
                for a in range(ppp):
                    m = h * ppp + a
                    if d > 0:
                        wait_slot(wbuf.at[m, band], wx_rsem.at[m])
                    for ch in range(chains):
                        @pl.when(m != i)
                        def _():
                            send_part(1, ch, m, nexts[ch])

                        @pl.when(m == i)
                        def _():
                            own_part(1, ch, nexts[ch])

        for ch in range(chains):
            if t > 1:
                now = one_block(rbuf[0, t, ch, j])
                for d in reach:
                    send_part(t, ch, lax.rem(i + d, pre), now)
                own_part(t, ch, now)
            for n in range(1, post * rep):
                spread_rates(t, ch, n).start()
        if t == 0:
            @pl.when(away)
            def _():
                wait_slot(sbuf.at[0], s_rsem.at[0])
                wait_slot(sbuf.at[1], s_rsem.at[1])
                wait_slot(ctbuf, s_rsem.at[2])

            types = ctbuf[...]
            gain = jnp.zeros(types.shape, F32)
            for k in range(gains_ref.shape[0]):
                gain = jnp.where(types == k, gains_ref[k], gain)
            gain = gain[0:1]
        for ch in range(chains):
            if t == 0:
                for m in range(pre):
                    @pl.when(jnp.logical_or(away, m != i))
                    def _():
                        wait_slot(precv.at[0, ch, m], p_rsem.at[0, ch, m])

            else:
                for d in range(1, pre):
                    m = lax.rem(i + d, pre)
                    wait_slot(precv.at[t, ch, m], p_rsem.at[t, ch, m])
            cur = precv[t, ch, 0].astype(F32)
            for m in range(1, pre):
                cur = cur + precv[t, ch, m].astype(F32)
            act = jnp.tanh(gain * cur + sbuf[0, ch].astype(F32))
            acts[t, ch] = act
            curs[t, ch] = cur
            fresh = ((1.0 - LEAK) * rbuf[0, t, ch, j].astype(F32) + LEAK * act).astype(BF16)
            if t < STEPS - 1:
                rbuf[0, t + 1, ch, j] = fresh
            else:
                fbuf[1, 0, 0, ch] = fresh

    errors = [sbuf[1, ch].astype(F32) for ch in range(chains)]
    tally = jnp.zeros((8, n_pre), F32)
    for t in reversed(range(STEPS)):
        for ch in range(chains):
            error = errors[ch]
            act = acts[t, ch]
            du = error * LEAK * (1.0 - act * act)
            delta = (du * gain).astype(BF16)
            if t > 0:
                dz[t, ch, i] = delta
                for d in reach:
                    gather_copy(t, ch, d).start()
            else:
                dsend[ch] = delta
                for m in range(pre):
                    @pl.when(jnp.logical_or(away, m != i))
                    def _():
                        delta_copy(0, ch, m).start()

                @pl.when(home)
                def _():
                    dbuf[0, a_me, 0, ch, j] = dsend[ch]

            weighed = du * curs[t, ch]
            for top in range(0, rh, 8):
                tally = tally + weighed[top:top + 8]
        if t == 0:
            break
        for ch in range(chains):
            back = None
            for d in range(pre):
                m = lax.rem(i + d, pre)
                if d > 0:
                    wait_slot(dz.at[t, ch, m], z_rsem.at[t, ch, m])
                term = lax.dot_general(
                    one_block(dz[t, ch, m]), wbuf[m], (((1,), (1,)), ((), ())), preferred_element_type=F32
                )
                back = term if back is None else back + term
            errors[ch] = (1.0 - LEAK) * errors[ch] + back
            for a in range(ppp):
                for n in range(1, post * rep):
                    spread_delta(t, ch, a, n).start()
                dbuf[0, a, t, ch, j] = dz[t, ch, j * ppp + a]

    kinds = grecv.shape[-1]
    hot = (lax.broadcasted_iota(jnp.int32, (kinds, n_pre), 0) == ctbuf[0:1]).astype(F32)
    grecv[me] = lax.dot_general(
        tally, hot, (((1,), (1,)), ((), ())), preferred_element_type=F32, precision=lax.Precision.HIGHEST
    )

    def gain_copy(n):
        return copy(grecv.at[me], grecv.at[me], g_sem.at[n], g_rsem.at[me], where_is(peer(n)))

    def send_gain(n, carry):
        gain_copy(n).start()
        return carry

    lax.fori_loop(1, group, send_gain, 0)

    for ch in range(chains):
        for m in range(pre):
            @pl.when(jnp.logical_or(away, m != i))
            def _():
                final_copy(ch, m).start()

        @pl.when(home)
        def _():
            fbuf[0, a_me, j, ch] = fbuf[1, 0, 0, ch]

    for t in range(STEPS):
        for ch in range(chains):
            for n in range(1, post * rep):
                h, side = cross(n)
                wait_slot(rbuf.at[side, t, ch, h], r_rsem.at[side, t, ch, h])
                if t > 0:
                    for a in range(ppp):
                        wait_slot(dbuf.at[side, a, t, ch, h], q_rsem.at[side, a, t, ch, h])

    def outer(side, low, high, a):
        lead = (high - low) * chains * post
        return lax.dot_general(
            flat_rows(rbuf[side, low:high], lead), flat_rows(dbuf[side, a, low:high], lead),
            (((0,), (0,)), ((), ())), preferred_element_type=F32,
        )

    for a in range(ppp):
        cols = slice(a * n_pre, (a + 1) * n_pre)
        g_ref[:, cols] = outer(0, 1, STEPS, a) + outer(1, 1, STEPS, a)
    for ch in range(chains):
        for a in range(ppp):
            for h in range(post):
                @pl.when(jnp.logical_not(is_me(ppp * j + a, h)))
                def _():
                    wait_slot(dbuf.at[0, a, 0, ch, h], d_rsem.at[ch, a, h])

            swap_delta(0, ch, a).start()
    for a in range(ppp):
        cols = slice(a * n_pre, (a + 1) * n_pre)
        for ch in range(chains):
            swap_delta(0, ch, a).wait_recv()
        g_ref[:, cols] += outer(0, 0, 1, a) + outer(1, 0, 1, a)

    for a in range(ppp):
        for h in range(post):
            for ch in range(chains):
                @pl.when(jnp.logical_not(is_me(ppp * j + a, h)))
                def _():
                    wait_slot(fbuf.at[0, a, h, ch], f_rsem.at[ch, a, h])

        final_ref[:, a * n_pre:(a + 1) * n_pre] = flat_rows(fbuf[0, a], post * chains)

    def take_gain(n, carry):
        source = peer(n)
        wait_slot(grecv.at[source], g_rsem.at[source])
        return carry

    lax.fori_loop(1, group, take_gain, 0)
    gathered = grecv[0]
    for n in range(1, group):
        gathered = gathered + grecv[n]
    gg_ref[...] = jnp.sum(gathered, axis=0, keepdims=True)[:, :gg_ref.shape[1]]

    for h in range(post):
        @pl.when(jnp.logical_and(home, h != j))
        def _():
            for one in share_copies(h):
                one.wait_send()

    for d in range(1, post):
        h = lax.rem(j + d, post)
        for a in range(ppp):
            weight_copy(d, a).wait_send()
            weight_swap(h, a).wait_send()
    for t in range(STEPS):
        for ch in range(chains):
            for d in reach:
                if t > 0:
                    part_copy(t, ch, lax.rem(i + d, pre)).wait_send()
                    gather_copy(t, ch, d).wait_send()
            for n in range(1, post * rep):
                spread_rates(t, ch, n).wait_send()
                if t > 0:
                    for a in range(ppp):
                        spread_delta(t, ch, a, n).wait_send()
    for ch in range(chains):
        for a in range(ppp):
            swap_delta(0, ch, a).wait_send()
            for h in range(post):
                @pl.when(jnp.logical_not(is_me(ppp * j + a, h)))
                def _():
                    first_copy(ch, a, h).wait_send()

        for m in range(pre):
            @pl.when(jnp.logical_or(away, m != i))
            def _():
                delta_copy(0, ch, m).wait_send()
                final_copy(ch, m).wait_send()

    def end_gain(n, carry):
        gain_copy(n).wait_send()
        return carry

    lax.fori_loop(1, group, end_gain, 0)


def body(rates0, stimulus, cotangent, weights, src_block, dst_block, live_count, cell_type, gains):
    pre, post, rep = lax.axis_size("pre"), lax.axis_size("post"), lax.axis_size("rep")
    batch, n_pre = rates0.shape
    n_post = stimulus.shape[1]
    slots, width = weights.shape[2], weights.shape[3]
    ppp = pre // post
    chains = 1
    rh = batch // (chains * post)
    group = pre * post * rep
    smem = pl.BlockSpec(memory_space=pltpu.SMEM)
    vmem = pl.BlockSpec(memory_space=pltpu.VMEM)

    dense = pl.pallas_call(
        build_kernel,
        grid=(slots // CHUNK,),
        out_shape=jax.ShapeDtypeStruct((ppp, n_pre, n_pre), BF16),
        in_specs=[smem, smem, smem, pl.BlockSpec((1, 1, CHUNK, width, width), lambda p: (0, 0, p, 0, 0))],
        out_specs=pl.BlockSpec((ppp, n_pre, n_pre), lambda p: (0, 0, 0)),
        scratch_shapes=[pltpu.VMEM((ppp, n_pre, n_pre), F32)],
        compiler_params=pltpu.CompilerParams(vmem_limit_bytes=32 * 2**20),
        name="dense_tile",
    )(src_block, dst_block, live_count, weights)

    dma = pltpu.SemaphoreType.DMA
    V = pltpu.VMEM
    final, gain_grad, dense_grad = pl.pallas_call(
        functools.partial(step_kernel, (pre, post, rep, chains, rh, n_pre)),
        out_shape=(
            jax.ShapeDtypeStruct((batch, n_post), BF16),
            jax.ShapeDtypeStruct((1, gains.shape[0]), F32),
            jax.ShapeDtypeStruct((n_pre, n_post), F32),
        ),
        in_specs=[vmem, vmem, vmem, vmem, vmem, smem],
        out_specs=(vmem, vmem, vmem),
        scratch_shapes=[
            V((pre, n_pre, n_pre), BF16),
            V((2, STEPS, chains, post, rh, n_pre), BF16),
            V((2, ppp, STEPS, chains, post, rh, n_pre), BF16),
            V((STEPS, chains, pre, rh, n_pre), BF16),
            V((2, ppp, post, chains, rh, n_pre), BF16),
            V((STEPS, chains, pre, rh, n_pre), BF16),
            V((STEPS, chains, pre, rh, n_pre), BF16),
            V((chains, rh, n_pre), BF16),
            V((2, post, chains, rh, n_pre), BF16),
            V((2, chains, rh, n_pre), BF16),
            V((8, n_pre), jnp.int32),
            V((8, n_pre), jnp.int32),
            V((group, 8, 128), F32),
            V((STEPS, chains, rh, n_pre), F32),
            V((STEPS, chains, rh, n_pre), F32),
            dma((post, ppp)), dma((pre,)), dma((pre,)), dma((pre,)),
            dma((post, 3)), dma((3,)),
            dma((STEPS, chains, pre)), dma((STEPS, chains, pre)),
            dma((STEPS, chains, post * rep)), dma((rep, STEPS, chains, post)),
            dma((STEPS, chains, pre)), dma((STEPS, chains, pre)),
            dma((STEPS, chains, ppp, post * rep)), dma((rep, ppp, STEPS, chains, post)),
            dma((chains, pre)), dma((chains, ppp, post)),
            dma((chains, pre)), dma((chains, ppp, post)),
            dma((chains, ppp)), dma((chains, ppp)),
            dma((group,)), dma((group,)),
        ],
        compiler_params=pltpu.CompilerParams(
            collective_id=0, has_side_effects=True, vmem_limit_bytes=48 * 2**20
        ),
        name="window",
    )(rates0, stimulus, cotangent, dense, cell_type.reshape(1, n_post), gains)

    share = slots // rep
    grad = pl.pallas_call(
        emit_kernel,
        out_shape=jax.ShapeDtypeStruct((1, 1, share, width, width), F32),
        in_specs=[smem, smem, smem, vmem],
        out_specs=pl.BlockSpec(memory_space=pl.ANY),
        scratch_shapes=[V((width, width), F32), dma((share,))],
        compiler_params=pltpu.CompilerParams(vmem_limit_bytes=32 * 2**20),
        name="emit_slots",
    )(src_block, dst_block, live_count, dense_grad)
    return final, grad, gain_grad.reshape(gains.shape)


def solution(mesh):
    return jax.shard_map(
        body,
        mesh=mesh,
        in_specs=(
            P(("groups", "rep"), "pre"),
            P(("groups", "rep"), "post"),
            P(("groups", "rep"), "post"),
            P(("groups", "pre"), "post", None, None, None),
            P(("groups", "pre"), "post", None),
            P(("groups", "pre"), "post", None),
            P(("groups", "pre"), "post"),
            P(("groups", "post")),
            P(),
        ),
        out_specs=(
            P(("groups", "rep"), "post"),
            P(("groups", "pre"), "post", "rep", None, None),
            P("groups"),
        ),
        check_vma=False,
    )
```

time: 79.1 us -> 74.7 us (0.944)
  Pallas kernels: 73.6 us -> 68.8 us
    pallas_call x1, Pallas kernels: 69.8 us -> 64.9 us  [body(): pl.pallas_call(functools.partial(step_kernel, (pre, post, rep, chains, rh...]
    unnamed x21 -> x22, local copies, waits for them, and re-layouts: 3.58 us -> 4.09 us
where the time goes in v2:
time: 74.7 us; the launch traced here: 74.3 us
  Pallas kernels  68.8 us (92%)
  local copies, waits for them, and re-layouts  4.09 us (5%)
  between operations  1.41 us (2%)
    pallas_call x1, Pallas kernels, body(): pl.pallas_call(functools.partial(step_kernel, (pre, post, rep, chains, rh...  64.9 us
    unnamed x22, local copies, waits for them, and re-layouts  4.09 us
    pallas_call x1, Pallas kernels, body(): pl.pallas_call(emit_kernel, out_shape=jax.ShapeDtypeStruct((1, 1, share,...  2.13 us
    pallas_call x1, Pallas kernels, body(): pl.pallas_call(build_kernel, grid=(slots // CHUNK,), out_shape=jax.ShapeD...  1.77 us

profile of v2, /device:TPU:3, one launch (start us, length us, event | category | flops | bytes accessed | tf_op | source)
XLA Modules:
  0.0 74.3 jit_solution(15545366376510558657)
XLA Ops:
  0.6 0.0 copy-start.9
  1.3 0.0 copy-start
  1.3 1.6 %copy-done = bf16[1,1,64,128,128]{4,3,2,1,0:T(8,128)(2,1)S(1)} copy-done((bf16[1,1,64,128,128]{4,3,2,1,0:T(8,128)(2,1)S(1)}, bf16[1,1,64,128,128]{4,3,2,1,0:T(8,128)(2,1)}, u32[]{:S(2)}) %copy-start) | copy-done | bytes 2097176
  2.9 0.0 copy-start.5
  2.9 0.7 copy-done.5
  3.6 0.0 copy-start.7
  3.6 0.7 copy-done.7
  4.2 0.0 copy-start.2
  4.2 0.0 copy-start.3
  4.2 0.0 copy-start.4
  4.2 0.0 copy-start.6
  4.2 0.0 copy-start.8
  4.2 1.8 %dense_tile.1.w_ref = bf16[2,512,512]{2,1,0:T(8,128)(2,1)S(1)} custom-call(s32[1,1,64]{2,1,0:T(1,128)S(1)} %copy-done.5, s32[1,1,64]{2,1,0:T(1,128)S(1)} %copy-done.7, s32[1,1]{1,0:T(1,128)S(6)} %copy.14.live_ref, bf16[1,1,64,128,128]{4,3,2,1,0:T(8,128)(2,1)S(1)} %copy-done), custom_call_target="tpu_custom_call" | custom-call | tf_op jit(solution)/shard_map/dense_tile/pallas_call | solution.py:510
  6.0 0.0 copy-done.9
  6.0 0.0 copy-done.1
  6.0 0.0 copy-done.2
  6.0 0.0 copy-done.3
  6.1 0.0 copy-done.4
  6.1 64.9 %window.1 = (bf16[64,1024]{1,0:T(8,128)(2,1)S(1)}, f32[1,32]{1,0:T(1,128)S(1)}, f32[512,1024]{1,0:T(8,128)S(1)}) custom-call(bf16[64,512]{1,0:T(8,128)(2,1)S(1)} %copy-done.3, bf16[64,1024]{1,0:T(8,128)(2,1)S(1)} %copy-done.1, bf16[64,1024]{1,0:T(8,128)(2,1)S(1)} %copy-done.2, bf16[2,512,512]{2,1,0:T(8,128)(2,1)S(1)} %dense_tile.1.w_ref, ...), custom_call_target="tpu_custom_call" | custom-call | tf_op jit(solution)/shard_map/window/pallas_call | solution.py:523
  71.0 0.0 copy-done.6
  71.0 0.0 copy-done.8
  71.0 2.1 %emit_slots.1 = f32[1,1,32,128,128]{4,3,2,1,0:T(8,128)} custom-call(s32[1,1,64]{2,1,0:T(1,128)S(1)} %copy-done.6, s32[1,1,64]{2,1,0:T(1,128)S(1)} %copy-done.8, s32[1,1]{1,0:T(1,128)S(6)} %copy.14.live_ref, f32[512,1024]{1,0:T(8,128)S(1)} %get-tuple-element.7.g_ref), custom_call_target="tpu_custom_call" | custom-call | tf_op jit(solution)/shard_map/emit_slots/pallas_call | solution.py:566
  73.1 0.7 copy.15
  73.8 0.5 copy.16
  (1 shorter events, 0.0 us)
Async XLA Ops:
  0.6 5.4 %copy-start.9 = (f32[32]{0:T(128)S(1)}, f32[32]{0:T(128)}, u32[]{:S(2)}) copy-start(f32[32]{0:T(128)} %gains_ref.1) | copy-start | bytes 388
  1.3 1.6 %copy-start = (bf16[1,1,64,128,128]{4,3,2,1,0:T(8,128)(2,1)S(1)}, bf16[1,1,64,128,128]{4,3,2,1,0:T(8,128)(2,1)}, u32[]{:S(2)}) copy-start(bf16[1,1,64,128,128]{4,3,2,1,0:T(8,128)(2,1)} %w_ref.1) | copy-start | bytes 6291460
  2.9 0.7 copy-start.5
  3.6 0.7 copy-start.7
  4.2 1.8 %copy-start.1 = (bf16[64,1024]{1,0:T(8,128)(2,1)S(1)}, bf16[64,1024]{1,0:T(8,128)(2,1)}, u32[]{:S(2)}) copy-start(bf16[64,1024]{1,0:T(8,128)(2,1)} %stim_ref.1) | copy-start | bytes 393220
  4.2 1.8 %copy-start.2 = (bf16[64,1024]{1,0:T(8,128)(2,1)S(1)}, bf16[64,1024]{1,0:T(8,128)(2,1)}, u32[]{:S(2)}) copy-start(bf16[64,1024]{1,0:T(8,128)(2,1)} %cot_ref.1) | copy-start | bytes 393220
  4.2 1.8 %copy-start.3 = (bf16[64,512]{1,0:T(8,128)(2,1)S(1)}, bf16[64,512]{1,0:T(8,128)(2,1)}, u32[]{:S(2)}) copy-start(bf16[64,512]{1,0:T(8,128)(2,1)} %rates_ref.1) | copy-start | bytes 196612
  4.2 1.8 %copy-start.4 = (s32[1024]{0:T(1024)S(1)}, s32[1024]{0:T(1024)}, u32[]{:S(2)}) copy-start(s32[1024]{0:T(1024)} %param.16) | copy-start | bytes 12292
  4.2 66.8 %copy-start.6 = (s32[1,1,64]{2,1,0:T(1,128)S(1)}, s32[1,1,64]{2,1,0:T(1,128)}, u32[]{:S(2)}) copy-start(s32[1,1,64]{2,1,0:T(1,128)} %src_ref.3) | copy-start | bytes 772
  4.2 66.8 %copy-start.8 = (s32[1,1,64]{2,1,0:T(1,128)S(1)}, s32[1,1,64]{2,1,0:T(1,128)}, u32[]{:S(2)}) copy-start(s32[1,1,64]{2,1,0:T(1,128)} %dst_ref.3) | copy-start | bytes 772

commit v3 on v2

--- a/solution.py
+++ b/solution.py
@@ -155,6 +155,10 @@
 
     pl.semaphore_wait(barrier, group - 1)
 
+    for d in range(1, post):
+        for a in range(ppp):
+            weight_copy(d, a).start()
+
     def share_copies(h):
         to = {"post": h}
         yield copy(stage.at[0, h], sbuf.at[0], s_sem.at[h, 0], s_rsem.at[0], to)
@@ -261,9 +265,6 @@
                             psend[0, ch, a * post + h] = value
                             first_copy(ch, a, h).start()
 
-            for d in range(1, post):
-                for a in range(ppp):
-                    weight_copy(d, a).start()
             for a in range(ppp):
                 wbuf[j * ppp + a] = w_ref[a]
         elif t == 1:
@@ -293,8 +294,9 @@
                 for d in reach:
                     send_part(t, ch, lax.rem(i + d, pre), now)
                 own_part(t, ch, now)
-            for n in range(1, post * rep):
-                spread_rates(t, ch, n).start()
+            for back in range(t + 1 if t == 2 else 0 if t < 2 else 1):
+                for n in range(1, post * rep):
+                    spread_rates(t - back, ch, n).start()
         if t == 0:
             @pl.when(away)
             def _():

time: 74.7 us -> 73.7 us (0.987)
  Pallas kernels: 68.8 us -> 67.4 us
    pallas_call x1, Pallas kernels: 64.9 us -> 63.1 us  [body(): pl.pallas_call(functools.partial(step_kernel, (pre, post, rep, chains, rh...]
where the time goes in v3:
time: 73.7 us; the launch traced here: 72.9 us
  Pallas kernels  67.4 us (91%)
  local copies, waits for them, and re-layouts  4.09 us (6%)
  between operations  1.41 us (2%)
    pallas_call x1, Pallas kernels, body(): pl.pallas_call(functools.partial(step_kernel, (pre, post, rep, chains, rh...  63.1 us
    unnamed x22, local copies, waits for them, and re-layouts  4.09 us
    pallas_call x1, Pallas kernels, body(): pl.pallas_call(build_kernel, grid=(slots // CHUNK,), out_shape=jax.ShapeD...  2.15 us
    pallas_call x1, Pallas kernels, body(): pl.pallas_call(emit_kernel, out_shape=jax.ShapeDtypeStruct((1, 1, share,...  2.13 us

profile of v3, /device:TPU:3, one launch (start us, length us, event | category | flops | bytes accessed | tf_op | source)
XLA Modules:
  0.0 72.9 jit_solution(1685941518302986177)
XLA Ops:
  0.6 0.0 copy-start.9
  1.3 0.0 copy-start
  1.3 1.6 %copy-done = bf16[1,1,64,128,128]{4,3,2,1,0:T(8,128)(2,1)S(1)} copy-done((bf16[1,1,64,128,128]{4,3,2,1,0:T(8,128)(2,1)S(1)}, bf16[1,1,64,128,128]{4,3,2,1,0:T(8,128)(2,1)}, u32[]{:S(2)}) %copy-start) | copy-done | bytes 2097176
  2.9 0.0 copy-start.5
  2.9 0.7 copy-done.5
  3.6 0.0 copy-start.7
  3.6 0.7 copy-done.7
  4.2 0.0 copy-start.1
  4.2 0.0 copy-start.2
  4.2 0.0 copy-start.3
  4.2 0.0 copy-start.6
  4.2 0.0 copy-start.8
  4.2 2.1 %dense_tile.1.w_ref = bf16[2,512,512]{2,1,0:T(8,128)(2,1)S(1)} custom-call(s32[1,1,64]{2,1,0:T(1,128)S(1)} %copy-done.5, s32[1,1,64]{2,1,0:T(1,128)S(1)} %copy-done.7, s32[1,1]{1,0:T(1,128)S(6)} %copy.14.live_ref, bf16[1,1,64,128,128]{4,3,2,1,0:T(8,128)(2,1)S(1)} %copy-done), custom_call_target="tpu_custom_call" | custom-call | tf_op jit(solution)/shard_map/dense_tile/pallas_call | solution.py:512
  6.4 0.0 copy-done.9
  6.4 0.0 copy-done.1
  6.4 0.0 copy-done.2
  6.4 0.0 copy-done.3
  6.4 0.0 copy-done.4
  6.4 63.1 %window.1 = (bf16[64,1024]{1,0:T(8,128)(2,1)S(1)}, f32[1,32]{1,0:T(1,128)S(1)}, f32[512,1024]{1,0:T(8,128)S(1)}) custom-call(bf16[64,512]{1,0:T(8,128)(2,1)S(1)} %copy-done.3, bf16[64,1024]{1,0:T(8,128)(2,1)S(1)} %copy-done.1, bf16[64,1024]{1,0:T(8,128)(2,1)S(1)} %copy-done.2, bf16[2,512,512]{2,1,0:T(8,128)(2,1)S(1)} %dense_tile.1.w_ref, ...), custom_call_target="tpu_custom_call" | custom-call | tf_op jit(solution)/shard_map/window/pallas_call | solution.py:525
  69.5 0.0 copy-done.6
  69.6 0.0 copy-done.8
  69.6 2.1 %emit_slots.1 = f32[1,1,32,128,128]{4,3,2,1,0:T(8,128)} custom-call(s32[1,1,64]{2,1,0:T(1,128)S(1)} %copy-done.6, s32[1,1,64]{2,1,0:T(1,128)S(1)} %copy-done.8, s32[1,1]{1,0:T(1,128)S(6)} %copy.14.live_ref, f32[512,1024]{1,0:T(8,128)S(1)} %get-tuple-element.7.g_ref), custom_call_target="tpu_custom_call" | custom-call | tf_op jit(solution)/shard_map/emit_slots/pallas_call | solution.py:568
  71.7 0.7 copy.15
  72.4 0.5 copy.16
  (1 shorter events, 0.0 us)
Async XLA Ops:
  0.6 5.8 %copy-start.9 = (f32[32]{0:T(128)S(1)}, f32[32]{0:T(128)}, u32[]{:S(2)}) copy-start(f32[32]{0:T(128)} %gains_ref.1) | copy-start | bytes 388
  1.3 1.6 %copy-start = (bf16[1,1,64,128,128]{4,3,2,1,0:T(8,128)(2,1)S(1)}, bf16[1,1,64,128,128]{4,3,2,1,0:T(8,128)(2,1)}, u32[]{:S(2)}) copy-start(bf16[1,1,64,128,128]{4,3,2,1,0:T(8,128)(2,1)} %w_ref.1) | copy-start | bytes 6291460
  2.9 0.7 copy-start.5
  3.6 0.7 copy-start.7
  4.2 2.2 %copy-start.1 = (bf16[64,1024]{1,0:T(8,128)(2,1)S(1)}, bf16[64,1024]{1,0:T(8,128)(2,1)}, u32[]{:S(2)}) copy-start(bf16[64,1024]{1,0:T(8,128)(2,1)} %stim_ref.1) | copy-start | bytes 393220
  4.2 2.2 %copy-start.2 = (bf16[64,1024]{1,0:T(8,128)(2,1)S(1)}, bf16[64,1024]{1,0:T(8,128)(2,1)}, u32[]{:S(2)}) copy-start(bf16[64,1024]{1,0:T(8,128)(2,1)} %cot_ref.1) | copy-start | bytes 393220
  4.2 2.2 %copy-start.3 = (bf16[64,512]{1,0:T(8,128)(2,1)S(1)}, bf16[64,512]{1,0:T(8,128)(2,1)}, u32[]{:S(2)}) copy-start(bf16[64,512]{1,0:T(8,128)(2,1)} %rates_ref.1) | copy-start | bytes 196612
  4.2 2.2 %copy-start.4 = (s32[1024]{0:T(1024)S(1)}, s32[1024]{0:T(1024)}, u32[]{:S(2)}) copy-start(s32[1024]{0:T(1024)} %param.16) | copy-start | bytes 12292
  4.2 65.3 %copy-start.6 = (s32[1,1,64]{2,1,0:T(1,128)S(1)}, s32[1,1,64]{2,1,0:T(1,128)}, u32[]{:S(2)}) copy-start(s32[1,1,64]{2,1,0:T(1,128)} %src_ref.3) | copy-start | bytes 772
  4.2 65.3 %copy-start.8 = (s32[1,1,64]{2,1,0:T(1,128)S(1)}, s32[1,1,64]{2,1,0:T(1,128)}, u32[]{:S(2)}) copy-start(s32[1,1,64]{2,1,0:T(1,128)} %dst_ref.3) | copy-start | bytes 772
